TPU v7x, 512 devices: a whole 4x8x8 slice. The times are simulated.
512 devices in a mesh: space: 32 (over z, x), brow: 8 (over y), bcol: 2 (over core).
Axes of the slice: x: 4, y: 8, z: 8, core: 2. Of those that a mesh axis runs over, the one named last changes fastest.
Arguments:
- orbitals: float32 [589824, 256], P(('space', 'brow'), 'bcol'), may hold values from -0.0078125 to 0.0078125
- applied: float32 [589824, 256], P(('space', 'brow'), 'bcol'), may hold values from -0.0078125 to 0.0078125
- cotangent: float32 [589824, 256], P(('space', 'brow'), 'bcol'), may hold values from -6 to 6
- rotation: float32 [256, 256], P('brow', 'bcol'), may hold values from -0.5 to 1.5, as said below
- levels: float32 [256], replicated, may hold values from -3 to 9.8, as said below
Outputs:
- orbital_grad: float32 [589824, 256], P(('space', 'brow'), 'bcol')
Inputs may be any that keep to these rules, and one draw needn't show every extreme that they name: rotation has a unit diagonal plus independent entries of deviation 0.4 / sqrt(256). levels rise with the index, neighbours at least 0.025 apart.
All inputs are finite; a program needn't handle non-finite values.
Results may differ from a plain program's by a relative error of at most 0.0003.
Values sent between devices are 32-bit elements; how exact they have to be, the bound alone decides.
No kernel may reach another device: no remote copies, remote signals or barrier semaphores. Data moves between devices by JAX's collectives and lax.ppermute only.
A program may use at most 64 MiB of HBM per device.

v0:
```python
import jax
import jax.numpy as jnp
from jax import lax
from jax.sharding import PartitionSpec as P


def matmul(left, right):
    return jnp.dot(left, right, preferred_element_type=jnp.float32, precision=lax.Precision.HIGHEST)


def inner_cells(left, right):
    return lax.dot_general(
        left,
        right,
        (((0,), (0,)), ((), ())),
        preferred_element_type=jnp.float32,
        precision=lax.Precision.HIGHEST,
    )


def outer_bands(left, right):
    return lax.dot_general(
        left,
        right,
        (((1,), (1,)), ((), ())),
        preferred_element_type=jnp.float32,
        precision=lax.Precision.HIGHEST,
    )


def subspace(rotation, levels, grad_rot):
    gram_rot = inner_cells(rotation, grad_rot)
    level_gaps = levels[None, :] - levels[:, None]
    diag_mask = jnp.eye(levels.shape[0], dtype=bool)
    inverse = jnp.where(
        diag_mask, jnp.float32(0.0), 1.0 / jnp.where(diag_mask, jnp.float32(1.0), level_gaps)
    )
    mixing = inverse * gram_rot
    sym_ham = mixing + mixing.T
    sym_ovl = mixing * levels[None, :] + levels[:, None] * mixing.T + jnp.diag(jnp.diag(gram_rot))
    ham_coef = outer_bands(matmul(rotation, sym_ham), rotation)
    ovl_coef = -outer_bands(matmul(rotation, sym_ovl), rotation)
    return (ham_coef, ovl_coef)


def band_plan(orbitals, applied, cotangent, row_panel, levels):
    band_width = orbitals.shape[1]
    band_first = lax.axis_index("bcol") * band_width
    orb_whole = lax.all_gather(orbitals, "bcol", axis=1, tiled=True)
    col_sums = lax.psum(inner_cells(orb_whole, cotangent), ("space", "brow"))
    grad_rot, full_rot = (
        lax.all_gather(col_sums, "bcol", axis=1, tiled=True),
        lax.all_gather(row_panel, "bcol", axis=1, tiled=True),
    )
    ham_coef, ovl_coef = subspace(full_rot, levels, grad_rot)
    app_whole, cot_whole = (
        lax.all_gather(applied, "bcol", axis=1, tiled=True),
        lax.all_gather(cotangent, "bcol", axis=1, tiled=True),
    )
    ovl_cols = lax.dynamic_slice_in_dim(ovl_coef, band_first, band_width, 1)
    ham_cols = lax.dynamic_slice_in_dim(ham_coef, band_first, band_width, 1)
    rot_rows = lax.dynamic_slice_in_dim(full_rot, band_first, band_width, 0)
    result = (
        matmul(orb_whole, ovl_cols) + matmul(app_whole, ham_cols) + outer_bands(cot_whole, rot_rows)
    )
    return result


def body(orbitals, applied, cotangent, rotation, levels):
    row_panel = lax.all_gather(rotation, "brow", axis=0, tiled=True)
    result = band_plan(orbitals, applied, cotangent, row_panel, levels)
    return result


def solution(mesh):
    return jax.shard_map(
        body,
        mesh=mesh,
        in_specs=(
            P(("space", "brow"), "bcol"),
            P(("space", "brow"), "bcol"),
            P(("space", "brow"), "bcol"),
            P("brow", "bcol"),
            P(),
        ),
        out_specs=P(("space", "brow"), "bcol"),
        check_vma=False,
    )
```

profile of v0, /device:TPU:1, one launch (start us, length us, event | category | flops | bytes accessed | tf_op | source)
XLA Modules:
  0.0 323.9 jit_solution(460007272820262635)
XLA Ops:
  6.5 0.0 copy-start.1
  6.5 0.0 all-gather.4.cloned.1.call-start
  6.5 0.7 all-gather.4.cloned.1.call-update
  7.3 0.0 all-reduce.2.cloned.1.call-start
  7.3 27.9 %all-gather.4.cloned.1.call-done = f32[2304,256]{1,0:T(8,128)} async-done(((f32[2304,128]{1,0:T(8,128)}), f32[2304,256]{1,0:T(8,128)}) %all-gather.4.cloned.1.call-update) | async-done | bytes 2359312 | tf_op jit(solution)/shard_map/all_gather | solution.py:49
  35.2 0.0 copy-done.1
  35.2 6.1 %fusion.20 = f32[256,128]{1,0:T(8,128)} fusion(f32[2304,256]{1,0:T(8,128)} %all-gather.4.cloned.1.call-done, f32[2304,128]{1,0:T(8,128)S(1)} %copy-done.1), kind=kOutput, calls=%fused_computation.29 | convolution fusion | flops 905969664 | bytes 3670016 | tf_op jit(solution)/shard_map/dot_general | solution.py:12
  41.4 0.0 all-reduce.2.cloned.1.call-update
  41.4 0.0 copy-start.2
  41.4 0.0 all-gather.6.cloned.1.call-start
  41.4 0.7 all-gather.6.cloned.1.call-update
  42.1 0.0 all-gather.8.cloned.1.call-start
  42.2 0.5 all-gather.8.cloned.1.call-update
  42.7 0.0 copy-done.2
  42.7 18.6 %all_gather.20 = f32[256,128]{1,0:T(8,128)S(1)} all-gather(f32[32,128]{1,0:T(8,128)S(1)} %copy-done.2), channel_id=1, replica_groups=mesh['space'=32,'brow'=8,'bcol'=2] {'brow'}, dimensions={0}, use_global_device_ids=true | all-gather | bytes 147456 | tf_op jit(solution)/shard_map/all_gather | solution.py:70
  61.4 7.9 %all_gather.21 = f32[256,256]{1,0:T(8,128)S(1)} all-gather(f32[256,128]{1,0:T(8,128)S(1)} %all_gather.20), channel_id=1, replica_groups=mesh['space'=32,'brow'=8,'bcol'=2] {'bcol'}, dimensions={1}, use_global_device_ids=true | all-gather | bytes 393216 | tf_op jit(solution)/shard_map/all_gather | solution.py:53
  69.2 197.0 %all-reduce.2.cloned.1.call-done = f32[256,128]{1,0:T(8,128)} async-done(((f32[256,128]{1,0:T(8,128)}), f32[256,128]{1,0:T(8,128)}) %all-reduce.2.cloned.1.call-update) | async-done | bytes 131088 | tf_op jit(solution)/shard_map/psum | solution.py:50
  266.3 7.2 %all_gather.19 = f32[256,256]{1,0:T(8,128)S(1)} all-gather(f32[256,128]{1,0:T(8,128)} %all-reduce.2.cloned.1.call-done), channel_id=1, replica_groups=mesh['space'=32,'brow'=8,'bcol'=2] {'bcol'}, dimensions={1}, use_global_device_ids=true | all-gather | bytes 393216 | tf_op jit(solution)/shard_map/all_gather | solution.py:52
  273.5 0.0 copy-start.3
  273.5 0.6 fusion.21
  274.1 0.1 copy.8
  274.2 2.3 gather_fusion
  276.6 0.0 copy-done.3
  276.6 0.7 fusion.3
  277.3 0.6 fusion.22
  277.9 0.0 copy-start
  277.9 0.7 fusion.1
  278.6 0.6 fusion.23
  279.2 0.3 copy-done
  279.6 2.6 fusion.9
  282.2 7.3 %all-gather.6.cloned.1.call-done = f32[2304,256]{1,0:T(8,128)} async-done(((f32[2304,128]{1,0:T(8,128)}), f32[2304,256]{1,0:T(8,128)}) %all-gather.6.cloned.1.call-update) | async-done | bytes 2359312 | tf_op jit(solution)/shard_map/all_gather | solution.py:57
  289.5 4.3 %convolution_add_fusion.1 = f32[128,2304]{1,0:T(8,128)S(1)} fusion(f32[128,2304]{1,0:T(8,128)S(1)} %fusion.9, f32[2304,256]{1,0:T(8,128)} %all-gather.6.cloned.1.call-done, f32[256,256]{1,0:T(8,128)S(1)} %fusion.23, s32[]{:T(128)S(6)} %select_n.34), kind=kOutput, calls=%fused_computation.2 | convolution fusion | flops 906264576 | bytes 4849668 | tf_op jit(solution)/shard_map/dot_general | solution.py:8
  293.8 18.0 %all-gather.8.cloned.1.call-done = f32[2304,256]{1,0:T(8,128)} async-done(((f32[2304,128]{1,0:T(8,128)}), f32[2304,256]{1,0:T(8,128)}) %all-gather.8.cloned.1.call-update) | async-done | bytes 2359312 | tf_op jit(solution)/shard_map/all_gather | solution.py:58
  311.8 4.2 %fusion = f32[2304,128]{0,1:T(8,128)S(1)} fusion(f32[128,2304]{1,0:T(8,128)S(1)} %convolution_add_fusion.1, f32[2304,256]{1,0:T(8,128)} %all-gather.8.cloned.1.call-done, f32[256,256]{1,0:T(8,128)S(1)} %all_gather.21, s32[]{:T(128)S(6)} %select_n.34), kind=kOutput, calls=%fused_computation.3 | convolution fusion | flops 906264576 | bytes 4849668 | tf_op jit(solution)/shard_map/dot_general | solution.py:22
  316.0 1.4 copy.9
  (1 shorter events, 0.0 us)
Async XLA Ops:
  6.5 28.7 %copy-start.1 = (f32[2304,128]{1,0:T(8,128)S(1)}, f32[2304,128]{1,0:T(8,128)}, u32[]{:S(2)}) copy-start(f32[2304,128]{1,0:T(8,128)} %param.7) | copy-start | bytes 3538948
  6.5 28.7 %all-gather.4.cloned.1.call-start = ((), (), s32[]{:S(2)}) async-start(), calls=%async_computation | async-start | bytes 3538944 | tf_op jit(solution)/shard_map/all_gather | solution.py:49
  7.3 259.0 %all-reduce.2.cloned.1.call-start = ((), (), s32[]{:S(2)}) async-start(), calls=%async_computation.1 | async-start | bytes 262144 | tf_op jit(solution)/shard_map/psum | solution.py:50
  41.4 1.3 copy-start.2
  41.4 248.1 %all-gather.6.cloned.1.call-start = ((), (), s32[]{:S(2)}) async-start(), calls=%async_computation.2 | async-start | bytes 3538944 | tf_op jit(solution)/shard_map/all_gather | solution.py:57
  42.1 269.6 %all-gather.8.cloned.1.call-start = ((), (), s32[]{:S(2)}) async-start(), calls=%async_computation.3 | async-start | bytes 3538944 | tf_op jit(solution)/shard_map/all_gather | solution.py:58
  273.5 3.1 copy-start.3
  277.9 1.7 copy-start
Sparse Core Ops, SparseCore 0:
  9.4 25.7 all-gather.3
  41.5 224.7 all-reduce.1
  268.5 20.8 all-gather.5
  291.6 20.1 all-gather.7
where the time goes:
time: 324 us
  waiting for transfers between devices  252 us (78%)
  blocking collectives  33.7 us (10%)
  matrix products  20.4 us (6%)
  between operations  13.2 us (4%)
  local copies, waits for them, and re-layouts  4.21 us (1%)
    psum x1, waiting for transfers between devices, band_plan(): col_sums = lax.psum(inner_cells(orb_whole, cotangent), ('space', 'brow'))  197 us
    all_gather x1, waiting for transfers between devices, band_plan(): orb_whole = lax.all_gather(orbitals, 'bcol', axis=1, tiled=True)  27.9 us
    all_gather x1, blocking collectives, body(): row_panel = lax.all_gather(rotation, 'brow', axis=0, tiled=True)  18.6 us
    all_gather x1, waiting for transfers between devices, band_plan(): lax.all_gather(cotangent, 'bcol', axis=1, tiled=True)  18 us
    dot_general x4, matrix products, matmul(): jnp.dot(left, right, preferred_element_type=jnp.float32, precision=lax.Pr...  8.33 us
    all_gather x1, blocking collectives, band_plan(): lax.all_gather(row_panel, 'bcol', axis=1, tiled=True)  7.88 us
    all_gather x1, waiting for transfers between devices, band_plan(): lax.all_gather(applied, 'bcol', axis=1, tiled=True)  7.28 us
    all_gather x1, blocking collectives, band_plan(): lax.all_gather(col_sums, 'bcol', axis=1, tiled=True)  7.22 us
  transfers between devices with their start and end apart: 4, of which 4 were waited for; matrix products, arithmetic and copies ran while one was open for 4% of the time, Pallas kernels for 0%

commit v1 on v0

--- a/solution.py
+++ b/solution.py
@@ -47,7 +47,7 @@
     band_width = orbitals.shape[1]
     band_first = lax.axis_index("bcol") * band_width
     orb_whole = lax.all_gather(orbitals, "bcol", axis=1, tiled=True)
-    col_sums = lax.psum(inner_cells(orb_whole, cotangent), ("space", "brow"))
+    col_sums = jnp.sum(lax.all_gather(inner_cells(orb_whole, cotangent), ("space", "brow")), axis=0)
     grad_rot, full_rot = (
         lax.all_gather(col_sums, "bcol", axis=1, tiled=True),
         lax.all_gather(row_panel, "bcol", axis=1, tiled=True),

time: 324 us -> 314 us (0.969)
  waiting for transfers between devices: 252 us -> 234 us
  other arithmetic: 0.01 us -> 12.2 us
  blocking collectives: 33.7 us -> 29.4 us
    psum x1 -> x0, waiting for transfers between devices: 197 us -> none  [band_plan(): col_sums = lax.psum(inner_cells(orb_whole, cotangent), ('space', 'brow'))]
    all_gather x0 -> x1, waiting for transfers between devices: none -> 190 us  [band_plan(): lax.all_gather(inner_cells(orb_whole, cotangent), ('space', 'brow'))]
    reduce_sum x0 -> x1, other arithmetic: none -> 12.2 us  [band_plan(): jnp.sum(lax.all_gather(inner_cells(orb_whole, cotangent), ('space', 'brow...]
    all_gather x1, waiting for transfers between devices: 7.28 us -> 0.02 us  [band_plan(): lax.all_gather(applied, 'bcol', axis=1, tiled=True)]
    all_gather x1, blocking collectives: 7.22 us -> 2.89 us  [band_plan(): lax.all_gather(col_sums, 'bcol', axis=1, tiled=True)]
    all_gather x1, waiting for transfers between devices: 18 us -> 14.3 us  [band_plan(): lax.all_gather(cotangent, 'bcol', axis=1, tiled=True)]
  transfers between devices with their start and end apart: 4 -> 4, of which waited for: 4 -> 3; matrix products, arithmetic and copies ran while one was open for 4% -> 8% of each run, Pallas kernels for 0% -> 0%
where the time goes in v1:
time: 314 us
  waiting for transfers between devices  234 us (75%)
  blocking collectives  29.4 us (9%)
  matrix products  20.5 us (7%)
  between operations  13.2 us (4%)
  other arithmetic  12.2 us (4%)
  local copies, waits for them, and re-layouts  4.21 us (1%)
    all_gather x1, waiting for transfers between devices, band_plan(): lax.all_gather(inner_cells(orb_whole, cotangent), ('space', 'brow'))  190 us
    all_gather x1, waiting for transfers between devices, band_plan(): orb_whole = lax.all_gather(orbitals, 'bcol', axis=1, tiled=True)  27.9 us
    all_gather x1, blocking collectives, body(): row_panel = lax.all_gather(rotation, 'brow', axis=0, tiled=True)  18.6 us
    all_gather x1, waiting for transfers between devices, band_plan(): lax.all_gather(cotangent, 'bcol', axis=1, tiled=True)  14.3 us
    reduce_sum x1, other arithmetic, band_plan(): jnp.sum(lax.all_gather(inner_cells(orb_whole, cotangent), ('space', 'brow...  12.2 us
    dot_general x4, matrix products, matmul(): jnp.dot(left, right, preferred_element_type=jnp.float32, precision=lax.Pr...  8.34 us
    all_gather x1, blocking collectives, band_plan(): lax.all_gather(row_panel, 'bcol', axis=1, tiled=True)  7.86 us
    dot_general x2, matrix products, inner_cells(): lax.dot_general(left, right, (((0,), (0,)), ((), ())), preferred_element_...  6.74 us
  transfers between devices with their start and end apart: 4, of which 3 were waited for; matrix products, arithmetic and copies ran while one was open for 8% of the time, Pallas kernels for 0%

profile of v1, /device:TPU:1, one launch (start us, length us, event | category | flops | bytes accessed | tf_op | source)
XLA Modules:
  0.0 313.6 jit_solution(12135250595857794140)
XLA Ops:
  6.5 0.0 copy-start.1
  6.5 0.0 all-gather.6.cloned.1.call-start
  6.5 0.7 all-gather.6.cloned.1.call-update
  7.3 0.0 all-gather.12.cloned.1.call-start
  7.3 27.9 %all-gather.6.cloned.1.call-done = f32[2304,256]{1,0:T(8,128)} async-done(((f32[2304,128]{1,0:T(8,128)}), f32[2304,256]{1,0:T(8,128)}) %all-gather.6.cloned.1.call-update) | async-done | bytes 2359312 | tf_op jit(solution)/shard_map/all_gather | solution.py:49
  35.2 0.0 copy-done.1
  35.2 6.1 %fusion.20 = f32[256,128]{1,0:T(8,128)} fusion(f32[2304,256]{1,0:T(8,128)} %all-gather.6.cloned.1.call-done, f32[2304,128]{1,0:T(8,128)S(1)} %copy-done.1), kind=kOutput, calls=%fused_computation.29 | convolution fusion | flops 905969664 | bytes 3670016 | tf_op jit(solution)/shard_map/dot_general | solution.py:12
  41.4 0.0 all-gather.12.cloned.1.call-update
  41.4 0.0 copy-start.2
  41.4 0.0 all-gather.8.cloned.1.call-start
  41.4 0.7 all-gather.8.cloned.1.call-update
  42.1 0.0 all-gather.10.cloned.1.call-start
  42.2 0.5 all-gather.10.cloned.1.call-update
  42.7 0.0 copy-done.2
  42.7 18.6 %all_gather.28 = f32[256,128]{1,0:T(8,128)S(1)} all-gather(f32[32,128]{1,0:T(8,128)S(1)} %copy-done.2), channel_id=1, replica_groups=mesh['space'=32,'brow'=8,'bcol'=2] {'brow'}, dimensions={0}, use_global_device_ids=true | all-gather | bytes 147456 | tf_op jit(solution)/shard_map/all_gather | solution.py:70
  61.4 7.9 %all_gather.29 = f32[256,256]{1,0:T(8,128)S(1)} all-gather(f32[256,128]{1,0:T(8,128)S(1)} %all_gather.28), channel_id=1, replica_groups=mesh['space'=32,'brow'=8,'bcol'=2] {'bcol'}, dimensions={1}, use_global_device_ids=true | all-gather | bytes 393216 | tf_op jit(solution)/shard_map/all_gather | solution.py:53
  69.2 189.8 %all-gather.12.cloned.1.call-done = f32[65536,128]{1,0:T(8,128)} async-done(((f32[256,128]{1,0:T(8,128)}), f32[65536,128]{1,0:T(8,128)}) %all-gather.12.cloned.1.call-update) | async-done | bytes 33554448 | tf_op jit(solution)/shard_map/all_gather | solution.py:50
  259.0 12.2 %reduce_sum.9 = f32[256,128]{1,0:T(8,128)S(1)} reduce(f32[256,256,128]{2,1,0:T(8,128)} %bitcast.25, f32[]{:T(128)} %constant.7.clone.1), dimensions={0}, to_apply=%region_0.0 | reduce | flops 8355840 | bytes 33685508 | tf_op jit(solution)/shard_map/reduce_sum | solution.py:50
  271.2 2.9 all_gather.27
  274.1 0.0 copy-start.3
  274.1 0.6 fusion.21
  274.7 0.1 copy.8
  274.9 2.3 gather_fusion
  277.2 0.0 copy-done.3
  277.2 0.7 fusion.3
  278.0 0.6 fusion.22
  278.6 0.0 copy-start
  278.6 0.7 fusion.1
  279.3 0.6 fusion.23
  279.9 0.3 copy-done
  280.2 2.6 fusion.9
  282.8 0.0 all-gather.8.cloned.1.call-done
  282.9 4.3 %convolution_add_fusion.1 = f32[128,2304]{1,0:T(8,128)S(1)} fusion(f32[128,2304]{1,0:T(8,128)S(1)} %fusion.9, f32[2304,256]{1,0:T(8,128)} %all-gather.8.cloned.1.call-done, f32[256,256]{1,0:T(8,128)S(1)} %fusion.23, s32[]{:T(128)S(6)} %select_n.34), kind=kOutput, calls=%fused_computation.2 | convolution fusion | flops 906264576 | bytes 4849668 | tf_op jit(solution)/shard_map/dot_general | solution.py:8
  287.2 14.3 %all-gather.10.cloned.1.call-done = f32[2304,256]{1,0:T(8,128)} async-done(((f32[2304,128]{1,0:T(8,128)}), f32[2304,256]{1,0:T(8,128)}) %all-gather.10.cloned.1.call-update) | async-done | bytes 2359312 | tf_op jit(solution)/shard_map/all_gather | solution.py:58
  301.5 4.2 %fusion = f32[2304,128]{0,1:T(8,128)S(1)} fusion(f32[128,2304]{1,0:T(8,128)S(1)} %convolution_add_fusion.1, f32[2304,256]{1,0:T(8,128)} %all-gather.10.cloned.1.call-done, f32[256,256]{1,0:T(8,128)S(1)} %all_gather.29, s32[]{:T(128)S(6)} %select_n.34), kind=kOutput, calls=%fused_computation.3 | convolution fusion | flops 906264576 | bytes 4849668 | tf_op jit(solution)/shard_map/dot_general | solution.py:22
  305.6 1.4 copy.9
  (1 shorter events, 0.0 us)
Async XLA Ops:
  6.5 28.7 %copy-start.1 = (f32[2304,128]{1,0:T(8,128)S(1)}, f32[2304,128]{1,0:T(8,128)}, u32[]{:S(2)}) copy-start(f32[2304,128]{1,0:T(8,128)} %param.7) | copy-start | bytes 3538948
  6.5 28.7 %all-gather.6.cloned.1.call-start = ((), (), s32[]{:S(2)}) async-start(), calls=%async_computation | async-start | bytes 3538944 | tf_op jit(solution)/shard_map/all_gather | solution.py:49
  7.3 251.8 %all-gather.12.cloned.1.call-start = ((), (), s32[]{:S(2)}) async-start(), calls=%async_computation.3 | async-start | bytes 33685504 | tf_op jit(solution)/shard_map/all_gather | solution.py:50
  41.4 1.3 copy-start.2
  41.4 241.5 %all-gather.8.cloned.1.call-start = ((), (), s32[]{:S(2)}) async-start(), calls=%async_computation.1 | async-start | bytes 3538944 | tf_op jit(solution)/shard_map/all_gather | solution.py:57
  42.1 259.3 %all-gather.10.cloned.1.call-start = ((), (), s32[]{:S(2)}) async-start(), calls=%async_computation.2 | async-start | bytes 3538944 | tf_op jit(solution)/shard_map/all_gather | solution.py:58
  274.1 3.1 copy-start.3
  278.6 1.7 copy-start
Sparse Core Ops, SparseCore 0:
  9.4 25.7 all-gather.5
  41.5 217.4 all-gather.11
  261.1 18.2 all-gather.7
  281.3 20.1 all-gather.9
